TPU v7x, 512 devices: a whole 4x4x16 slice. The times are simulated.
512 devices in a mesh: seq: 64 (over y, z), cand: 8 (over x, core).
Axes of the slice: x: 4, y: 4, z: 16, core: 2. Of those that a mesh axis runs over, the one named last changes fastest.
Arguments:
- candidates: bfloat16 [2, 1024, 256], P(None, ('seq', 'cand')), may hold values from -30 to 30
- history: bfloat16 [2, 65536, 256], P(None, ('seq', 'cand')), may hold values from -30 to 30
- lengths: int32 [2], replicated, may hold values from 6553 to 65536, as said below
- w_query: bfloat16 [256, 256], replicated, may hold values from -0.525 to 0.525
- w_key: bfloat16 [256, 256], replicated, may hold values from -0.525 to 0.525
- w_value: bfloat16 [256, 256], replicated, may hold values from -0.375 to 0.375
- norm_gain: float32 [256], replicated, may hold values from 0.3 to 3
- w_out: bfloat16 [256, 256], replicated, may hold values from -0.375 to 0.375
Outputs:
- interest: bfloat16 [2, 1024, 256], P(None, ('seq', 'cand'))
Inputs may be any that keep to these rules, and one draw needn't show every extreme that they name: User u's valid history is its first lengths[u] slots; some user fills all 65536.
All inputs are finite; a program needn't handle non-finite values.
Results may differ from a plain program's by a relative error of at most 0.019.
Values may be sent and summed in bfloat16 or wider, within the bound.
No kernel may reach another device: no remote copies, remote signals or barrier semaphores. Data moves between devices by JAX's collectives and lax.ppermute only.
A program may use at most 64 MiB of HBM per device.

v0:
```python
import math

import jax
import jax.numpy as jnp
from jax import lax
from jax.sharding import PartitionSpec as P

HEAD_DIM = 32


def merged(array, axis, combine):
    everything = jax.tree.map(
        lambda part, kind: lax.all_gather(part.astype(kind), axis),
        array,
        (jnp.bfloat16, jnp.bfloat16, jnp.bfloat16),
    )

    def take(k):
        return jax.tree.map(lambda part, own: part[k].astype(own.dtype), everything, array)

    return lax.fori_loop(
        1, lax.axis_size(axis), lambda k, so_far: combine(so_far, take(k)), take(0)
    )


def spread_heads(matrix, factor, head_dim):
    split_shape = matrix.shape[:-1] + (matrix.shape[-1] // head_dim, head_dim)
    return (matrix.reshape(split_shape) * factor[..., None]).reshape(matrix.shape)


def shards(candidates, history, lengths, w_query, w_key, w_value, norm_gain, w_out):
    user_count, cand_dev, feature_width = candidates.shape
    inner_width = w_query.shape[1]
    head_dim = HEAD_DIM
    head_count = inner_width // head_dim
    score_scale = 1.0 / math.sqrt(head_dim)
    own_queries = jnp.dot(
        candidates.reshape(user_count * cand_dev, feature_width),
        w_query,
        preferred_element_type=jnp.float32,
    )
    own_queries = own_queries.astype(jnp.bfloat16).reshape(user_count, cand_dev, inner_width)
    queries = lax.all_gather(own_queries, "seq", axis=1, tiled=True)
    keyval_weight = jnp.concatenate([w_key, w_value], axis=1)
    row_piece = lax.all_gather(history, "cand", axis=1, tiled=True)
    row_count = row_piece.shape[1]
    product = jnp.dot(
        row_piece.reshape(user_count * row_count, feature_width),
        keyval_weight,
        preferred_element_type=jnp.float32,
    )
    keyval = product.astype(jnp.bfloat16).reshape(user_count, row_count, 2 * inner_width)
    block_rows = keyval.shape[1]
    first_row = lax.axis_index("seq") * block_rows
    positions = first_row + jnp.arange(block_rows, dtype=jnp.int32)
    row_valid = positions[None, :] < lengths[:, None]
    cand_block = queries.shape[1]
    step_size = math.gcd(cand_block, 64)

    def attend(user_items):
        query_user, keyval_user, valid_user = user_items
        key_heads = keyval_user[:, :inner_width].reshape(block_rows, head_count, head_dim)
        value_heads = keyval_user[:, inner_width:].reshape(block_rows, head_count, head_dim)
        mask_rows = valid_user[None, None, :]

        def attend_block(query_part):
            query_heads = query_part.reshape(step_size, head_count, head_dim)
            scores = (
                jnp.einsum(
                    "chd,rhd->chr", query_heads, key_heads, preferred_element_type=jnp.float32
                )
                * score_scale
            )
            scores = jnp.where(mask_rows, scores, jnp.float32(-1e30))
            peaks_local = jnp.max(scores, axis=2)
            exponent = jnp.where(
                mask_rows, jnp.exp(scores - peaks_local[:, :, None]), jnp.float32(0.0)
            )
            row_total = jnp.sum(exponent, axis=2)
            numerator = jnp.einsum(
                "chr,rhd->chd",
                exponent.astype(jnp.bfloat16),
                value_heads,
                preferred_element_type=jnp.float32,
            )
            return (peaks_local, row_total, numerator.reshape(step_size, inner_width))

        grouped = query_user.reshape(cand_block // step_size, step_size, inner_width)
        part_peaks, part_totals, part_numers = lax.map(attend_block, grouped)
        return (
            part_peaks.reshape(cand_block, head_count),
            part_totals.reshape(cand_block, head_count),
            part_numers.reshape(cand_block, inner_width),
        )

    peaks, totals, numerators = lax.map(attend, (queries, keyval, row_valid))
    own_index = lax.axis_index("seq")

    def join(left_part, right_part):
        joint_peak = jnp.maximum(left_part[0], right_part[0])
        left_factor = jnp.exp(left_part[0] - joint_peak)
        right_factor = jnp.exp(right_part[0] - joint_peak)
        joint_total = left_part[1] * left_factor + right_part[1] * right_factor
        joint_numer = spread_heads(left_part[2], left_factor, head_dim) + spread_heads(
            right_part[2], right_factor, head_dim
        )
        return (joint_peak, joint_total, joint_numer)

    merged_peak, merged_total, merged_numer = merged((peaks, totals, numerators), "seq", join)
    total_own = lax.dynamic_slice_in_dim(merged_total, own_index * cand_dev, cand_dev, 1)
    numer_own = lax.dynamic_slice_in_dim(merged_numer, own_index * cand_dev, cand_dev, 1)
    attended = spread_heads(numer_own, 1.0 / total_own, head_dim)
    normed = (
        attended
        * lax.rsqrt(jnp.mean(attended * attended, axis=-1, keepdims=True) + 1e-06)
        * norm_gain
    )
    normed = normed.astype(jnp.bfloat16)
    result = jnp.dot(
        normed.reshape(user_count * cand_dev, inner_width),
        w_out,
        preferred_element_type=jnp.float32,
    )
    return result.astype(jnp.bfloat16).reshape(user_count, cand_dev, feature_width)


def solution(mesh):
    placed = (
        P(None, ("seq", "cand"), None),
        P(None, ("seq", "cand"), None),
        P(),
        P(),
        P(),
        P(),
        P(),
        P(),
    )
    return jax.shard_map(
        shards,
        mesh=mesh,
        in_specs=placed,
        out_specs=P(None, ("seq", "cand"), None),
        check_vma=False,
    )
```

profile of v0, /device:TPU:6, one launch (start us, length us, event | category | flops | bytes accessed | tf_op | source)
XLA Modules:
  0.0 381.7 jit_solution(13332695501955855586)
XLA Ops:
  8.2 106.3 %all_gather.24 = bf16[2,128,256]{2,0,1:T(2,128)(2,1)S(1)} all-gather(bf16[2,2,256]{2,0,1:T(2,128)(2,1)S(1)} %copy.43), channel_id=1, replica_groups=mesh['seq'=64,'cand'=8] {'seq'}, dimensions={1}, use_global_device_ids=true | all-gather | bytes 133120 | tf_op jit(solution)/shard_map/all_gather | solution.py:43
  115.9 2.1 convolution_convert_fusion
  118.0 1.5 copy.60
  119.5 15.2 %while.48 = (s32[]{:T(128)}, bf16[2,128,8]{1,2,0:T(8,128)(2,1)S(1)}, bf16[2,128,8]{1,2,0:T(8,128)(2,1)S(1)}, bf16[2,128,256]{2,1,0:T(8,128)(2,1)}, bf16[2,128,25...) while((s32[]{:T(128)}, ...), condition=%wide.region_5.6_spmd, body=%wide.region_0.5_spmd.sunk | while | flops 73923584 | bytes 12164471 | solution.py:96
  120.4 1.3 dynamic-slice_bitcast_fusion.5
  121.8 4.5 %while.50 = (s32[]{:T(128)}, bf16[2,64,8]{1,0,2:T(2,128)(2,1)S(1)}, bf16[2,64,8]{1,0,2:T(2,128)(2,1)S(1)}, bf16[2,64,256]{2,1,0:T(8,128)(2,1)S(1)}, pred[1,1,102...) while((s32[]{:T(128)}, bf16[2,64,8]{1,0,2:T(2,128)(2,1)S(1)}, ...), condition=%wide.region_4.4_spmd, body=%wide.region_1.3_spmd.sunk | while | flops 73923584 | bytes 7689350 | solution.py:89
  128.0 1.3 dynamic-slice_bitcast_fusion.5
  129.4 4.5 %while.50 = (s32[]{:T(128)}, bf16[2,64,8]{1,0,2:T(2,128)(2,1)S(1)}, bf16[2,64,8]{1,0,2:T(2,128)(2,1)S(1)}, bf16[2,64,256]{2,1,0:T(8,128)(2,1)S(1)}, pred[1,1,102...) while((s32[]{:T(128)}, bf16[2,64,8]{1,0,2:T(2,128)(2,1)S(1)}, ...), condition=%wide.region_4.4_spmd, body=%wide.region_1.3_spmd.sunk | while | flops 73923584 | bytes 7689350 | solution.py:89
  134.8 81.0 %all-gather = bf16[128,128,8]{1,2,0:T(8,128)(2,1)S(1)} all-gather(bf16[2,128,8]{1,2,0:T(8,128)(2,1)S(1)} %get-tuple-element.265), channel_id=2, replica_groups=mesh['seq'=64,'cand'=8] {'seq'}, dimensions={0}, use_global_device_ids=true | all-gather | bytes 266240 | tf_op jit(solution)/shard_map/all_gather | solution.py:13
  215.8 79.7 %all-gather.1 = bf16[128,128,8]{1,2,0:T(8,128)(2,1)S(1)} all-gather(bf16[2,128,8]{1,2,0:T(8,128)(2,1)S(1)} %get-tuple-element.266), channel_id=3, replica_groups=mesh['seq'=64,'cand'=8] {'seq'}, dimensions={0}, use_global_device_ids=true | all-gather | bytes 266240 | tf_op jit(solution)/shard_map/all_gather | solution.py:13
  295.5 0.9 slice_convert_fusion
  296.6 76.8 %while.49 = (s32[]{:T(128)}, f32[2,128,8]{1,2,0:T(8,128)S(1)}, f32[2,128,8]{1,2,0:T(8,128)S(1)}, f32[2,128,256]{1,2,0:T(8,128)S(1)}, bf16[64,2,128,8]{2,3,1,0:T(...) while((s32[]{:T(128)}, f32[2,128,8]{1,2,0:T(8,128)S(1)}, ...), condition=%wide.region_7.8_spmd, body=%wide.region_6.7_spmd.sunk | while | flops 278533 | bytes 1253519 | solution.py:21
  296.7 0.9 constant_dynamic-slice_fusion.7
  297.9 0.9 constant_dynamic-slice_fusion.7
  299.1 0.9 constant_dynamic-slice_fusion.7
  300.3 0.9 constant_dynamic-slice_fusion.7
  301.6 0.9 constant_dynamic-slice_fusion.7
  302.8 0.9 constant_dynamic-slice_fusion.7
  304.0 0.9 constant_dynamic-slice_fusion.7
  305.2 0.9 constant_dynamic-slice_fusion.7
  306.4 0.9 constant_dynamic-slice_fusion.7
  307.7 0.9 constant_dynamic-slice_fusion.7
  308.9 0.9 constant_dynamic-slice_fusion.7
  310.1 0.9 constant_dynamic-slice_fusion.7
  311.3 0.9 constant_dynamic-slice_fusion.7
  312.5 0.9 constant_dynamic-slice_fusion.7
  313.7 0.9 constant_dynamic-slice_fusion.7
  315.0 0.9 constant_dynamic-slice_fusion.7
  316.2 0.9 constant_dynamic-slice_fusion.7
  317.4 0.9 constant_dynamic-slice_fusion.7
  318.6 0.9 constant_dynamic-slice_fusion.7
  319.8 0.9 constant_dynamic-slice_fusion.7
  (328 shorter events, 72.8 us)
Async XLA Ops:
  6.5 1.5 copy-start
  6.5 109.3 %all-gather.6.cloned.1.call-start = ((), (), s32[]{:S(2)}) async-start(), calls=%async_computation | async-start | bytes 1179648 | tf_op jit(solution)/shard_map/all_gather | solution.py:45
  7.3 288.3 %all-gather.8.cloned.1.call-start = ((), (), s32[]{:S(2)}) async-start(), calls=%async_computation.1 | async-start | bytes 8519680 | tf_op jit(solution)/shard_map/all_gather | solution.py:13
  296.6 77.4 %copy-start.2 = (f32[256]{0:T(256)S(1)}, f32[256]{0:T(256)}, u32[]{:S(2)}) copy-start(f32[256]{0:T(256)} %param.20) | copy-start | bytes 3076
  296.6 77.5 %copy-start.1 = (bf16[256,256]{1,0:T(8,128)(2,1)S(1)}, bf16[256,256]{1,0:T(8,128)(2,1)}, u32[]{:S(2)}) copy-start(bf16[256,256]{1,0:T(8,128)(2,1)} %param.21) | copy-start | bytes 393220
Sparse Core Ops, SparseCore 0:
  9.5 34.1 all-gather.5
  134.9 152.7 all-gather.7
where the time goes:
time: 383 us; the launch traced here: 382 us
  blocking collectives  267 us (70%)
  local copies, waits for them, and re-layouts  76.9 us (20%)
  between operations  13.5 us (4%)
  other arithmetic  13.3 us (3%)
  matrix products  7.41 us (2%)
    all_gather x2, blocking collectives, merged(): lax.all_gather(part.astype(kind), axis)  161 us
    all_gather x1, blocking collectives, shards(): queries = lax.all_gather(own_queries, 'seq', axis=1, tiled=True)  106 us
    dynamic_slice x126, local copies, waits for them, and re-layouts, take(): part[k].astype(own.dtype)  65.5 us
  transfers between devices with their start and end apart: 2, of which 0 were waited for; matrix products, arithmetic and copies ran while one was open for 1% of the time, Pallas kernels for 0%

commit v1 on v0

v1 whole, which is shorter than its diff:
```python
import functools
import math

import jax
import jax.numpy as jnp
from jax import lax
from jax.experimental import pallas as pl
from jax.experimental.pallas import tpu as pltpu
from jax.sharding import PartitionSpec as P

HEAD_DIM = 32
LANES = 128
SLOT = 16
EXPONENT = math.log2(math.e) / math.sqrt(HEAD_DIM)
NT = (((1,), (1,)), ((), ()))


def parts_of(array, count):
    pieces = []
    for _ in range(count):
        piece = array.astype(jnp.bfloat16).astype(jnp.float32)
        pieces.append(piece)
        array = array - piece
    return pieces


def attend_kernel(
    length_ref, cand_ref, history_ref, wq_ref, wk_ref, wv_ref, out_ref, cand_wide, out_wide
):
    users, rows, width = history_ref.shape
    devices = cand_ref.shape[0] // 8
    own = 2
    heads = width // HEAD_DIM
    cands = devices * own
    first_row = lax.axis_index("seq") * rows
    cand_wide[...] = cand_ref[...].astype(jnp.float32)
    out_wide[...] = jnp.zeros_like(out_wide)
    head_of_lane = lax.broadcasted_iota(jnp.int32, (cands, width), 1) // HEAD_DIM
    row_index = lax.broadcasted_iota(jnp.int32, (rows, width), 0)
    lane_index = lax.broadcasted_iota(jnp.int32, (width, rows), 1)
    for user in range(users):
        valid = length_ref[user] - first_row
        history = history_ref[user]
        keys = jnp.dot(history, wk_ref[...], preferred_element_type=jnp.float32)
        keys = jnp.where(row_index < valid, keys, keys[0:1]).astype(jnp.bfloat16)
        values = lax.dot_general(
            wv_ref[...], history, (((0,), (1,)), ((), ())), preferred_element_type=jnp.float32
        )
        values = jnp.where(lane_index < valid, values, 0.0).astype(jnp.bfloat16)
        ones = jnp.where(lane_index[:16] < valid, 1.0, 0.0).astype(jnp.bfloat16)
        halves = [
            jnp.concatenate(
                [
                    cand_wide[pl.ds((user * own + i) * 2 + half, devices, stride=8), :]
                    for half in range(2)
                ],
                axis=1,
            )
            for i in range(own)
        ]
        candidates = jnp.concatenate(halves, axis=0).astype(jnp.bfloat16)
        queries = jnp.dot(candidates, wq_ref[...], preferred_element_type=jnp.float32)
        queries = queries.astype(jnp.bfloat16).astype(jnp.float32)
        numerators, peaks, totals = [], [], []
        for pair in range(heads // 2):
            both = jnp.concatenate(
                [
                    jnp.where(head_of_lane == 2 * pair + k, queries, 0.0).astype(jnp.bfloat16)
                    for k in range(2)
                ],
                axis=0,
            )
            scores = lax.dot_general(keys, both, NT, preferred_element_type=jnp.float32)
            peak = jnp.max(scores, axis=0, keepdims=True)
            exps = jnp.exp2((scores - peak) * EXPONENT).astype(jnp.bfloat16)
            pair_values = jnp.concatenate(
                [values[2 * pair * HEAD_DIM : 2 * (pair + 1) * HEAD_DIM], ones], axis=0
            )
            sums = jnp.dot(pair_values, exps, preferred_element_type=jnp.float32)
            for k in range(2):
                lanes = slice(k * cands, (k + 1) * cands)
                numerators.append(sums[k * HEAD_DIM : (k + 1) * HEAD_DIM, lanes])
                peaks.append(peak[:, lanes])
                totals.append(sums[2 * HEAD_DIM : 2 * HEAD_DIM + 1, lanes])
        peak = jnp.where(valid > 0, jnp.concatenate(peaks, axis=0), -1e30)
        total = jnp.concatenate(totals, axis=0)
        pieces = parts_of(peak, 3) + parts_of(total, 2)
        filler = jnp.zeros((LANES - len(pieces) * heads, cands), jnp.float32)
        block = jnp.concatenate(numerators + pieces + [filler], axis=0)
        for part in range(3):
            turned = block[part * LANES : (part + 1) * LANES].T
            for i in range(own):
                out_wide[pl.ds((user * own + i) * 3 + part, devices, stride=SLOT), :] = turned[
                    i * devices : (i + 1) * devices
                ]
    out_ref[...] = out_wide[...].astype(jnp.bfloat16)


def join_kernel(part_ref, gain_ref, wout_ref, out_ref, wide):
    width = wout_ref.shape[0]
    heads = width // HEAD_DIM
    devices = part_ref.shape[0] // SLOT
    own_count = out_ref.shape[0]
    wide[...] = part_ref[...].astype(jnp.float32)

    def rows(own, part):
        return wide[pl.ds(own * 3 + part, devices, stride=SLOT), :]

    lane = lax.broadcasted_iota(jnp.int32, (LANES, 2 * width), 0)
    column = lax.broadcasted_iota(jnp.int32, (LANES, 2 * width), 1)
    is_peak = column < width
    head = jnp.where(is_peak, column, column - width) // HEAD_DIM
    same = (lane % heads == head) & (
        (is_peak & (lane < 3 * heads))
        | (~is_peak & (lane >= 3 * heads) & (lane < 5 * heads))
    )
    spread = jnp.where(same, 1.0, 0.0).astype(jnp.bfloat16)
    stats = jnp.concatenate([rows(own, 2) for own in range(own_count)], axis=0)
    stats = jnp.dot(stats.astype(jnp.bfloat16), spread, preferred_element_type=jnp.float32)
    attended = []
    for own in range(own_count):
        peak = stats[own * devices : (own + 1) * devices, :width]
        total = stats[own * devices : (own + 1) * devices, width:]
        joint = jnp.max(peak, axis=0, keepdims=True)
        factor = jnp.exp2((peak - joint) * EXPONENT)
        numerator = jnp.concatenate([rows(own, 0), rows(own, 1)], axis=1)
        numerator = jnp.sum(numerator * factor, axis=0, keepdims=True)
        attended.append(numerator / jnp.sum(total * factor, axis=0, keepdims=True))
    attended = jnp.concatenate(attended, axis=0)
    normed = (
        attended
        * lax.rsqrt(jnp.mean(attended * attended, axis=-1, keepdims=True) + 1e-06)
        * gain_ref[...]
    )
    out_ref[...] = jnp.dot(
        normed.astype(jnp.bfloat16), wout_ref[...], preferred_element_type=jnp.float32
    ).astype(jnp.bfloat16)


def shards(seq_count, candidates, history, lengths, w_query, w_key, w_value, norm_gain, w_out):
    users, own, width = candidates.shape
    vmem = pl.BlockSpec(memory_space=pltpu.VMEM)
    smem = pl.BlockSpec(memory_space=pltpu.SMEM)
    rows = lax.all_gather(history, "cand", axis=1, tiled=True)
    copies = jnp.broadcast_to(candidates.reshape(1, 8, LANES), (seq_count, 8, LANES))
    gathered = lax.all_to_all(copies, "seq", 0, 0, tiled=True).reshape(seq_count * 8, LANES)
    partial = pl.pallas_call(
        attend_kernel,
        out_shape=jax.ShapeDtypeStruct((seq_count * SLOT, LANES), jnp.bfloat16),
        in_specs=[smem] + [vmem] * 5,
        out_specs=vmem,
        scratch_shapes=[
            pltpu.VMEM((seq_count * 8, LANES), jnp.float32),
            pltpu.VMEM((seq_count * SLOT, LANES), jnp.float32),
        ],
        compiler_params=pltpu.CompilerParams(vmem_limit_bytes=48 * 1024 * 1024),
        name="attend",
    )(lengths, gathered, rows, w_query, w_key, w_value)
    partial = lax.all_to_all(partial.reshape(seq_count, SLOT, LANES), "seq", 0, 0, tiled=True)
    result = pl.pallas_call(
        join_kernel,
        out_shape=jax.ShapeDtypeStruct((users * own, width), jnp.bfloat16),
        in_specs=[vmem] * 3,
        out_specs=vmem,
        scratch_shapes=[pltpu.VMEM((seq_count * SLOT, LANES), jnp.float32)],
        compiler_params=pltpu.CompilerParams(vmem_limit_bytes=16 * 1024 * 1024),
        name="join",
    )(partial.reshape(seq_count * SLOT, LANES), norm_gain.reshape(1, width), w_out)
    return result.reshape(users, own, width)


def solution(mesh):
    split = P(None, ("seq", "cand"), None)
    return jax.shard_map(
        functools.partial(shards, mesh.shape["seq"]),
        mesh=mesh,
        in_specs=(split, split) + (P(),) * 6,
        out_specs=split,
        check_vma=False,
    )
```

time: 383 us -> 99 us (0.26)
  blocking collectives: 267 us -> 71.5 us
  local copies, waits for them, and re-layouts: 76.9 us -> 2.56 us
  other arithmetic: 13.3 us -> 0 us
  Pallas kernels: 0 us -> 7.63 us
  matrix products: 7.41 us -> 0 us
    all_gather x3 -> x0, blocking collectives: 267 us -> none  [the longest x2 161 us: merged(): lax.all_gather(part.astype(kind), axis)]
    all_to_all x0 -> x2, blocking collectives: none -> 71.5 us  [the longest x1 36.5 us: shards(): lax.all_to_all(partial.reshape(seq_count, SLOT, LANES), 'seq', 0, 0, tile...]
    dynamic_slice x136 -> x0, local copies, waits for them, and re-layouts: 67.8 us -> none  [the longest x126 65.5 us: take(): part[k].astype(own.dtype)]
    add x127 -> x0, other arithmetic: 8.82 us -> none  [the longest x63 7.56 us: join(): spread_heads(left_part[2], left_factor, head_dim)]
    pallas_call x0 -> x2, Pallas kernels: none -> 7.63 us  [the longest x1 7.15 us: shards(): pl.pallas_call(attend_kernel, out_shape=jax.ShapeDtypeStruct((seq_count *...]
    dot_general x11 -> x0, matrix products: 7.41 us -> none  [the longest x4 2.68 us: attend_block(): jnp.einsum('chr,rhd->chd', exponent.astype(jnp.bfloat16), value_heads, pr...]
  transfers between devices with their start and end apart: 2 -> 1, of which waited for: 0 -> 1; matrix products, arithmetic and copies ran while one was open for 1% -> 0% of each run, Pallas kernels for 0% -> 0%
where the time goes in v1:
time: 99 us; the launch traced here: 97.2 us
  blocking collectives  71.5 us (72%)
  between operations  13.5 us (14%)
  Pallas kernels  7.63 us (8%)
  local copies, waits for them, and re-layouts  2.56 us (3%)
  waiting for transfers between devices  2.06 us (2%)
    all_to_all x1, blocking collectives, shards(): lax.all_to_all(partial.reshape(seq_count, SLOT, LANES), 'seq', 0, 0, tile...  36.5 us
    all_to_all x1, blocking collectives, shards(): lax.all_to_all(copies, 'seq', 0, 0, tiled=True)  35 us
    pallas_call x1, Pallas kernels, shards(): pl.pallas_call(attend_kernel, out_shape=jax.ShapeDtypeStruct((seq_count *...  7.15 us
  transfers between devices with their start and end apart: 1, of which 1 were waited for; matrix products, arithmetic and copies ran while one was open for 0% of the time, Pallas kernels for 0%

profile of v1, /device:TPU:6, one launch (start us, length us, event | category | flops | bytes accessed | tf_op | source)
XLA Modules:
  0.0 97.2 jit_solution(7979100342928573207)
XLA Ops:
  6.5 0.0 copy-start.7
  6.5 0.0 all-gather.2.cloned.1.call-start
  6.5 0.7 all-gather.2.cloned.1.call-update
  7.3 0.0 copy-done.7
  7.3 0.0 copy-start.4
  7.3 0.0 copy-start.2
  7.3 0.0 copy-start.3
  7.3 35.0 %all_to_all.10 = bf16[64,8,128]{2,1,0:T(8,128)(2,1)S(1)} all-to-all(bf16[64,8,128]{2,1,0:T(8,128)(2,1)S(1)} %broadcast_in_dim.8), channel_id=1, replica_groups=mesh['seq'=64,'cand'=8] {'seq'}, dimensions={0} | all-to-all | bytes 262144 | tf_op jit(solution)/shard_map/all_to_all | solution.py:146
  42.4 0.0 copy-start.6
  42.4 1.4 %all-gather.2.cloned.1.call-done.history_ref = bf16[2,1024,256]{2,1,0:T(8,128)(2,1)} async-done(((bf16[2,128,256]{2,1,0:T(8,128)(2,1)}), bf16[2,1024,256]{2,1,0:T(8,128)(2,1)}) %all-gather.2.cloned.1.call-update) | async-done | bytes 1048592 | tf_op jit(solution)/shard_map/all_gather | solution.py:144
  43.7 0.0 copy-done.4
  43.7 0.0 copy-done.2
  43.7 0.0 copy-done.3
  43.7 0.0 copy-done.6
  43.7 0.0 copy-start
  43.7 1.2 %copy-done = bf16[2,1024,256]{2,1,0:T(8,128)(2,1)S(1)} copy-done((bf16[2,1024,256]{2,1,0:T(8,128)(2,1)S(1)}, bf16[2,1024,256]{2,1,0:T(8,128)(2,1)}, u32[]{:S(2)}) %copy-start) | copy-done | bytes 1048600
  45.0 7.1 %attend.1 = bf16[1024,128]{1,0:T(8,128)(2,1)S(1)} custom-call(s32[2]{0:T(128)S(1)} %copy-done.6, bf16[512,128]{1,0:T(8,128)(2,1)S(1)} %bitcast.6, bf16[2,1024,256]{2,1,0:T(8,128)(2,1)S(1)} %copy-done, bf16[256,256]{1,0:T(8,128)(2,1)S(1)} %copy-done.2, bf16[256,256]{1,0:T(8,128)(2,1)S(1)} %copy-done.3, bf16[256,256]{1,0:T(8,128)(2,1)S(1)} %copy-done.4), custom_call_target="tpu_custom_call" | custom-call | tf_op jit(solution)/shard_map/attend/pallas_call | solution.py:147
  52.1 0.0 copy-start.1
  52.1 36.5 %all_to_all.11 = bf16[64,16,128]{2,1,0:T(8,128)(2,1)S(1)} all-to-all(bf16[64,16,128]{2,1,0:T(8,128)(2,1)S(1)} %bitcast.5), channel_id=1, replica_groups=mesh['seq'=64,'cand'=8] {'seq'}, dimensions={0} | all-to-all | bytes 524288 | tf_op jit(solution)/shard_map/all_to_all | solution.py:159
  88.6 0.0 copy-start.5
  88.6 0.0 copy-done.1
  88.6 0.7 copy-done.5
  89.3 0.5 join.1
  89.8 0.6 reshape.21
  (2 shorter events, 0.0 us)
Async XLA Ops:
  6.5 0.7 copy-start.7
  6.5 37.2 %all-gather.2.cloned.1.call-start = ((), (), s32[]{:S(2)}) async-start(), calls=%async_computation.2 | async-start | bytes 1179648 | tf_op jit(solution)/shard_map/all_gather | solution.py:144
  7.3 36.4 %copy-start.4 = (bf16[256,256]{1,0:T(8,128)(2,1)S(1)}, bf16[256,256]{1,0:T(8,128)(2,1)}, u32[]{:S(2)}) copy-start(bf16[256,256]{1,0:T(8,128)(2,1)} %wv_ref.1) | copy-start | bytes 393220
  7.3 36.4 %copy-start.2 = (bf16[256,256]{1,0:T(8,128)(2,1)S(1)}, bf16[256,256]{1,0:T(8,128)(2,1)}, u32[]{:S(2)}) copy-start(bf16[256,256]{1,0:T(8,128)(2,1)} %wq_ref.1) | copy-start | bytes 393220
  7.3 36.4 %copy-start.3 = (bf16[256,256]{1,0:T(8,128)(2,1)S(1)}, bf16[256,256]{1,0:T(8,128)(2,1)}, u32[]{:S(2)}) copy-start(bf16[256,256]{1,0:T(8,128)(2,1)} %wk_ref.1) | copy-start | bytes 393220
  42.4 1.4 %copy-start.6 = (s32[2]{0:T(128)S(1)}, s32[2]{0:T(128)}, u32[]{:S(2)}) copy-start(s32[2]{0:T(128)} %length_ref.1) | copy-start | bytes 28
  43.7 1.2 %copy-start = (bf16[2,1024,256]{2,1,0:T(8,128)(2,1)S(1)}, bf16[2,1024,256]{2,1,0:T(8,128)(2,1)}, u32[]{:S(2)}) copy-start(bf16[2,1024,256]{2,1,0:T(8,128)(2,1)} %all-gather.2.cloned.1.call-done.history_ref) | copy-start | bytes 3145732
  52.1 36.5 %copy-start.1 = (bf16[256,256]{1,0:T(8,128)(2,1)S(1)}, bf16[256,256]{1,0:T(8,128)(2,1)}, u32[]{:S(2)}) copy-start(bf16[256,256]{1,0:T(8,128)(2,1)} %wout_ref.1) | copy-start | bytes 393220
  88.6 0.7 copy-start.5
Sparse Core Ops, SparseCore 0:
  9.5 34.1 all-gather.1

commit v2 on v1

v2 whole, which is shorter than its diff:
```python
import functools
import math

import jax
import jax.numpy as jnp
from jax import lax
from jax.experimental import pallas as pl
from jax.experimental.pallas import tpu as pltpu
from jax.sharding import Mesh, PartitionSpec as P

HEAD_DIM = 32
LANES = 128
SLOT = 10
STATS = 64
EXPONENT = math.log2(math.e) / math.sqrt(HEAD_DIM)
NT = (((1,), (1,)), ((), ()))
ONES = 16


def parts_of(array, count):
    pieces = []
    for _ in range(count):
        piece = array.astype(jnp.bfloat16).astype(jnp.float32)
        pieces.append(piece)
        array = array - piece
    return pieces


def project_kernel(side, length_ref, *refs):
    history_refs, (wk_ref, wv_ref, keys_ref, values_ref) = refs[:-4], refs[-4:]
    chips, users, block, width = history_refs[0].shape
    rows = len(history_refs) * chips * block
    first_row = lax.axis_index("seq") * 2 * rows
    core = (lax.axis_index("core") + side) % 2

    def position(shape, dimension):
        index = lax.broadcasted_iota(jnp.int32, shape, dimension)
        return (index // block) * (2 * block) + core * block + index % block

    row_index = position((rows, width), 0)
    lane_index = position((width + ONES, rows), 1)
    for user in range(users):
        valid = length_ref[user] - first_row
        history = jnp.concatenate(
            [ref[:, user].reshape(chips * block, width) for ref in history_refs], axis=0
        )
        keys = jnp.dot(history, wk_ref[...], preferred_element_type=jnp.float32)
        keys_ref[user] = jnp.where(row_index < valid, keys, keys[0:1]).astype(jnp.bfloat16)
        values = lax.dot_general(
            wv_ref[...], history, (((0,), (1,)), ((), ())), preferred_element_type=jnp.float32
        )
        values = jnp.concatenate([values, jnp.ones((ONES, rows), jnp.float32)], axis=0)
        values_ref[user] = jnp.where(lane_index < valid, values, 0.0).astype(jnp.bfloat16)


def attend_kernel(cand_ref, keys0, values0, keys1, values1, wq_ref, out_ref, cand_wide, out_wide):
    users, _, width = keys0.shape
    devices = cand_ref.shape[0] // 8
    own = 2
    heads = width // HEAD_DIM
    cands = devices * own
    cand_wide[...] = cand_ref[...].astype(jnp.float32)
    head_of_lane = lax.broadcasted_iota(jnp.int32, (cands, width), 1) // HEAD_DIM
    for user in range(users):
        halves = [(keys0, values0), (keys1, values1)]
        any_valid = [values[user, width : width + 1, 0:1] > 0.0 for _, values in halves]
        keys = [
            jnp.where(any_valid[k], halves[k][0][user], halves[1 - k][0][user, 0:1])
            for k in range(2)
        ]
        candidates = [
            jnp.concatenate(
                [
                    cand_wide[pl.ds((user * own + i) * 2 + half, devices, stride=8), :]
                    for half in range(2)
                ],
                axis=1,
            )
            for i in range(own)
        ]
        candidates = jnp.concatenate(candidates, axis=0).astype(jnp.bfloat16)
        queries = jnp.dot(candidates, wq_ref[...], preferred_element_type=jnp.float32)
        queries = queries.astype(jnp.bfloat16).astype(jnp.float32)
        numerators, peaks, totals = [], [], []
        for pair in range(heads // 2):
            both = jnp.concatenate(
                [
                    jnp.where(head_of_lane == 2 * pair + k, queries, 0.0).astype(jnp.bfloat16)
                    for k in range(2)
                ],
                axis=0,
            )
            scores = [
                lax.dot_general(part, both, NT, preferred_element_type=jnp.float32)
                for part in keys
            ]
            peak = jnp.max(jnp.maximum(scores[0], scores[1]), axis=0, keepdims=True)
            sums = 0.0
            for part, (_, values) in zip(scores, halves):
                exps = jnp.exp2((part - peak) * EXPONENT).astype(jnp.bfloat16)
                pair_values = jnp.concatenate(
                    [
                        values[user, 2 * pair * HEAD_DIM : 2 * (pair + 1) * HEAD_DIM],
                        values[user, width:],
                    ],
                    axis=0,
                )
                sums += jnp.dot(pair_values, exps, preferred_element_type=jnp.float32)
            for k in range(2):
                lanes = slice(k * cands, (k + 1) * cands)
                numerators.append(sums[k * HEAD_DIM : (k + 1) * HEAD_DIM, lanes])
                peaks.append(peak[:, lanes])
                totals.append(sums[2 * HEAD_DIM : 2 * HEAD_DIM + 1, lanes])
        total = jnp.concatenate(totals, axis=0)
        peak = jnp.where(total > 0.0, jnp.concatenate(peaks, axis=0), -1e30)
        pieces = parts_of(peak, 3) + parts_of(total, 2)
        filler = jnp.zeros((STATS - len(pieces) * heads, cands), jnp.float32)
        block = jnp.concatenate(numerators, axis=0)
        for half in range(2):
            turned = block[half * LANES : (half + 1) * LANES].T
            for i in range(own):
                row = (user * own + i) * 2 + half
                out_wide[pl.ds(row, devices, stride=SLOT), :] = turned[
                    i * devices : (i + 1) * devices
                ]
        stats = jnp.concatenate(pieces + [filler], axis=0)
        stats = jnp.concatenate(
            [stats[:, i * devices : (i + 1) * devices] for i in range(own)], axis=0
        )
        out_wide[pl.ds(2 * users * own + user, devices, stride=SLOT), :] = stats.T
    out_ref[...] = out_wide[...].astype(jnp.bfloat16)


def join_kernel(part_ref, gain_ref, wout_ref, out_ref, wide):
    width = wout_ref.shape[0]
    heads = width // HEAD_DIM
    devices = part_ref.shape[0] // SLOT
    users, own = out_ref.shape[:2]
    own_count = users * own
    wide[...] = part_ref[...].astype(jnp.float32)

    def rows(index):
        return wide[pl.ds(index, devices, stride=SLOT), :]

    lane = lax.broadcasted_iota(jnp.int32, (LANES, 2 * own * width), 0)
    column = lax.broadcasted_iota(jnp.int32, (LANES, 2 * own * width), 1)
    piece = lane % STATS // heads
    is_total = column // width % 2
    same = (
        (lane // STATS == column // (2 * width))
        & (lane % heads == column % width // HEAD_DIM)
        & (piece >= 3 * is_total)
        & (piece < 3 + 2 * is_total)
    )
    spread = jnp.where(same, 1.0, 0.0).astype(jnp.bfloat16)
    stats = jnp.concatenate([rows(2 * own_count + user) for user in range(users)], axis=0)
    stats = jnp.dot(stats.astype(jnp.bfloat16), spread, preferred_element_type=jnp.float32)
    attended = []
    for user in range(users):
        for i in range(own):
            both = stats[user * devices : (user + 1) * devices]
            peak = both[:, 2 * i * width : (2 * i + 1) * width]
            total = both[:, (2 * i + 1) * width : (2 * i + 2) * width]
            joint = jnp.max(peak, axis=0, keepdims=True)
            factor = jnp.exp2((peak - joint) * EXPONENT)
            index = 2 * (user * own + i)
            numerator = jnp.concatenate([rows(index), rows(index + 1)], axis=1)
            numerator = jnp.sum(numerator * factor, axis=0, keepdims=True)
            attended.append(numerator / jnp.sum(total * factor, axis=0, keepdims=True))
    attended = jnp.concatenate(attended, axis=0)
    normed = (
        attended
        * lax.rsqrt(jnp.mean(attended * attended, axis=-1, keepdims=True) + 1e-06)
        * gain_ref[...]
    )
    result = jnp.dot(
        normed.astype(jnp.bfloat16), wout_ref[...], preferred_element_type=jnp.float32
    )
    for user in range(users):
        out_ref[user] = result[user * own : (user + 1) * own].astype(jnp.bfloat16)


def shards(seq_count, candidates, history, lengths, w_query, w_key, w_value, norm_gain, w_out):
    users, own, width = candidates.shape
    vmem = pl.BlockSpec(memory_space=pltpu.VMEM)
    smem = pl.BlockSpec(memory_space=pltpu.SMEM)
    copies = jnp.broadcast_to(candidates.reshape(1, 8, LANES), (seq_count, 8, LANES))
    gathered = lax.all_to_all(copies, "seq", 0, 0, tiled=True).reshape(seq_count * 8, LANES)
    mine = lax.all_gather(history, "x", axis=0)
    half = mine.shape[0] // 2
    theirs = [
        lax.ppermute(part, "core", [(0, 1), (1, 0)]) for part in (mine[:half], mine[half:])
    ]
    rows = mine.shape[0] * mine.shape[2]

    def project(side, *history):
        return pl.pallas_call(
            functools.partial(project_kernel, side),
            out_shape=(
                jax.ShapeDtypeStruct((users, rows, width), jnp.bfloat16),
                jax.ShapeDtypeStruct((users, width + ONES, rows), jnp.bfloat16),
            ),
            in_specs=[smem] + [vmem] * (len(history) + 2),
            out_specs=(vmem, vmem),
            compiler_params=pltpu.CompilerParams(vmem_limit_bytes=24 * 1024 * 1024),
            name="project",
        )(lengths, *history, w_key, w_value)

    keys0, values0 = project(0, mine)
    keys1, values1 = project(1, *theirs)
    partial = pl.pallas_call(
        attend_kernel,
        out_shape=jax.ShapeDtypeStruct((seq_count * SLOT, LANES), jnp.bfloat16),
        in_specs=[vmem] * 6,
        out_specs=vmem,
        scratch_shapes=[
            pltpu.VMEM((seq_count * 8, LANES), jnp.float32),
            pltpu.VMEM((seq_count * SLOT, LANES), jnp.float32),
        ],
        compiler_params=pltpu.CompilerParams(vmem_limit_bytes=32 * 1024 * 1024),
        name="attend",
    )(gathered, keys0, values0, keys1, values1, w_query)
    partial = partial.reshape(seq_count, SLOT // 2, 2, LANES)
    partial = lax.all_to_all(partial, "seq", 0, 0, tiled=True)
    return pl.pallas_call(
        join_kernel,
        out_shape=jax.ShapeDtypeStruct((users, own, width), jnp.bfloat16),
        in_specs=[vmem] * 3,
        out_specs=vmem,
        scratch_shapes=[pltpu.VMEM((seq_count * SLOT, LANES), jnp.float32)],
        compiler_params=pltpu.CompilerParams(vmem_limit_bytes=16 * 1024 * 1024),
        name="join",
    )(partial.reshape(seq_count * SLOT, LANES), norm_gain.reshape(1, width), w_out)


def solution(mesh):
    split = P(None, ("seq", "x", "core"), None)
    seq, cand = mesh.shape["seq"], mesh.shape["cand"]
    finer = Mesh(mesh.devices.reshape(seq, cand // 2, 2), ("seq", "x", "core"))
    return jax.shard_map(
        functools.partial(shards, seq),
        mesh=finer,
        in_specs=(split, split) + (P(),) * 6,
        out_specs=split,
        check_vma=False,
    )
```

time: 99 us -> 79.9 us (0.81); the launches traced: 97.2 us -> 79.6 us
  blocking collectives: 71.5 us -> 45.9 us
  starting transfers between devices: 0.01 us -> 23.3 us
  between operations: 13.5 us -> 0.14 us
  waiting for transfers between devices: 2.06 us -> 0.1 us
    all_to_all x2 -> x1, blocking collectives: 71.5 us -> 32.5 us  [shards(): partial = lax.all_to_all(partial, 'seq', 0, 0, tiled=True)]
    all_to_all x0 -> x1, starting transfers between devices: none -> 18.9 us  [shards(): lax.all_to_all(copies, 'seq', 0, 0, tiled=True)]
    all_gather x0 -> x1, blocking collectives: none -> 13.4 us  [shards(): mine = lax.all_gather(history, 'x', axis=0)]
    ppermute x0 -> x2, starting transfers between devices: none -> 4.46 us  [shards(): lax.ppermute(part, 'core', [(0, 1), (1, 0)])]
    pallas_call x1 -> x3, Pallas kernels: 0.48 us -> 3.08 us  [the longest x2 1.97 us: project(): pl.pallas_call(functools.partial(project_kernel, side), out_shape=(jax.Sh...]
    pallas_call x1, Pallas kernels: 7.15 us -> 4.99 us  [shards(): pl.pallas_call(attend_kernel, out_shape=jax.ShapeDtypeStruct((seq_count *...]
    all_gather x1 -> x0, waiting for transfers between devices: 1.35 us -> none  [shards(): rows = lax.all_gather(history, 'cand', axis=1, tiled=True)]
    broadcast_in_dim x2, local copies, waits for them, and re-layouts: 0.03 us -> 1.36 us  [shards(): jnp.broadcast_to(candidates.reshape(1, 8, LANES), (seq_count, 8, LANES))]
  transfers between devices with their start and end apart: 1 -> 3, of which waited for: 1 -> 1; matrix products, arithmetic and copies ran while one was open for 0% -> 0% of each run, Pallas kernels for 0% -> 2%
where the time goes in v2:
time: 79.9 us; the launch traced here: 79.6 us
  blocking collectives  45.9 us (57%)
  starting transfers between devices  23.3 us (29%)
  Pallas kernels  8.07 us (10%)
  local copies, waits for them, and re-layouts  2.1 us (3%)
    all_to_all x1, blocking collectives, shards(): partial = lax.all_to_all(partial, 'seq', 0, 0, tiled=True)  32.5 us
    all_to_all x1, starting transfers between devices, shards(): lax.all_to_all(copies, 'seq', 0, 0, tiled=True)  18.9 us
    all_gather x1, blocking collectives, shards(): mine = lax.all_gather(history, 'x', axis=0)  13.4 us
    pallas_call x1, Pallas kernels, shards(): pl.pallas_call(attend_kernel, out_shape=jax.ShapeDtypeStruct((seq_count *...  4.99 us
    ppermute x2, starting transfers between devices, shards(): lax.ppermute(part, 'core', [(0, 1), (1, 0)])  4.46 us
    pallas_call x2, Pallas kernels, project(): pl.pallas_call(functools.partial(project_kernel, side), out_shape=(jax.Sh...  1.97 us
  transfers between devices with their start and end apart: 3, of which 1 were waited for; matrix products, arithmetic and copies ran while one was open for 0% of the time, Pallas kernels for 2%

profile of v2, /device:TPU:6, one launch (start us, length us, event | category | flops | bytes accessed | tf_op | source)
XLA Modules:
  0.0 79.6 jit_solution(16687718035791598278)
XLA Ops:
  0.0 0.7 broadcast_in_dim.7
  0.7 0.7 broadcast_in_dim.8
  1.4 0.0 copy-start.6
  1.4 18.9 %all-to-all-start = ((bf16[64,8,128]{2,1,0:T(8,128)(2,1)}), bf16[64,8,128]{2,1,0:T(8,128)(2,1)S(1)}, u32[]{:S(2)}, u32[]{:S(2)}) async-start(bf16[64,8,128]{2,1,0:T(8,128)(2,1)} %broadcast_in_dim.8), calls=%async_computation | async-start | bytes 262144 | tf_op jit(solution)/shard_map/all_to_all | solution.py:188
  20.2 0.0 copy-done.6
  20.2 13.4 %all-gather = bf16[8,128,256]{2,1,0:T(8,128)(2,1)S(1)} all-gather(bf16[2,128,256]{2,1,0:T(8,128)(2,1)S(1)} %copy-done.6), channel_id=2, replica_groups=mesh['seq'=64,'x'=4,'core'=2] {'x'}, dimensions={0}, use_global_device_ids=true | all-gather | bytes 655360 | tf_op jit(solution)/shard_map/all_gather | solution.py:189
  33.6 0.0 copy-start
  33.6 0.0 copy-start.1
  33.7 2.1 %collective-permute-start = (bf16[2,2,128,256]{3,2,1,0:T(8,128)(2,1)S(1)}, bf16[2,2,128,256]{3,2,1,0:T(8,128)(2,1)S(1)}, u32[]{:S(2)}, u32[]{:S(2)}) collective-permute-start(bf16[2,2,128,256]{3,2,1,0:T(8,128)(2,1)S(1)} %bitcast.13), channel_id=1, source_target_pairs={{0,1},{1,0},{2,3},{3,2},{4,5},{5,4},{6,7},{7,6},{8,9},{9,8},{10,11... | collective-permute-start | bytes 786440 | tf_op jit(solution)/shard_map/ppermute | solution.py:192
  35.7 0.0 copy-start.4
  35.8 2.4 %collective-permute-start.1 = (bf16[2,2,128,256]{3,2,1,0:T(8,128)(2,1)S(1)}, bf16[2,2,128,256]{3,2,1,0:T(8,128)(2,1)S(1)}, u32[]{:S(2)}, u32[]{:S(2)}) collective-permute-start(bf16[2,2,128,256]{3,2,1,0:T(8,128)(2,1)S(1)} %bitcast.12), channel_id=1, source_target_pairs={{0,1},{1,0},{2,3},{3,2},{4,5},{5,4},{6,7},{7,6},{8,9},{9,8},{10,11... | collective-permute-start | bytes 786440 | tf_op jit(solution)/shard_map/ppermute | solution.py:192
  38.2 0.0 copy-done
  38.2 0.0 copy-done.1
  38.2 0.0 copy-done.4
  38.2 1.0 %project.2 = (bf16[2,512,256]{2,1,0:T(8,128)(2,1)S(1)}, bf16[2,272,512]{2,1,0:T(8,128)(2,1)S(1)}) custom-call(s32[2]{0:T(128)S(1)} %copy-done.4, bf16[4,2,128,256]{3,2,1,0:T(8,128)(2,1)S(1)} %bitcast.7, bf16[256,256]{1,0:T(8,128)(2,1)S(1)} %copy-done, bf16[256,256]{1,0:T(8,128)(2,1)S(1)} %copy-done.1), custom_call_target="tpu_custom_call" | custom-call | tf_op jit(solution)/shard_map/project/pallas_call | solution.py:197
  39.2 0.0 copy-start.2
  39.2 0.0 collective-permute-done.refs_0_
  39.2 0.1 collective-permute-done.1.refs_1_
  39.3 1.0 %project.3 = (bf16[2,512,256]{2,1,0:T(8,128)(2,1)S(1)}, bf16[2,272,512]{2,1,0:T(8,128)(2,1)S(1)}) custom-call(s32[2]{0:T(128)S(1)} %copy-done.4, bf16[2,2,128,256]{3,2,1,0:T(8,128)(2,1)S(1)} %collective-permute-done.refs_0_, bf16[2,2,128,256]{3,2,1,0:T(8,128)(2,1)S(1)} %collective-permute-done.1.refs_1_, bf16[256,256]{1,0:T(8,128)(2,1)S(1)} %copy-done, ...), custom_call_target="tpu_custom_call" | custom-call | tf_op jit(solution)/shard_map/project/pallas_call | solution.py:197
  40.3 0.0 all-to-all-done
  40.3 0.0 copy-done.2
  40.3 5.0 %attend.1 = bf16[640,128]{1,0:T(8,128)(2,1)S(1)} custom-call(bf16[512,128]{1,0:T(8,128)(2,1)S(1)} %bitcast.10, bf16[2,512,256]{2,1,0:T(8,128)(2,1)S(1)} %get-tuple-element.9.keys0, bf16[2,272,512]{2,1,0:T(8,128)(2,1)S(1)} %get-tuple-element.10.values0, bf16[2,512,256]{2,1,0:T(8,128)(2,1)S(1)} %get-tuple-element.11.keys1, ...), custom_call_target="tpu_custom_call" | custom-call | tf_op jit(solution)/shard_map/attend/pallas_call | solution.py:211
  45.3 0.0 copy-start.3
  45.3 32.5 %all_to_all.10 = bf16[64,5,2,128]{3,2,1,0:T(2,128)(2,1)S(1)} all-to-all(bf16[64,5,2,128]{3,2,1,0:T(2,128)(2,1)S(1)} %bitcast.8), channel_id=1, replica_groups=mesh['seq'=64,'x'=4,'core'=2] {'seq'}, dimensions={0} | all-to-all | bytes 327680 | tf_op jit(solution)/shard_map/all_to_all | solution.py:224
  77.8 0.0 copy-start.5
  77.8 0.0 copy-done.3
  77.8 0.7 copy-done.5
  78.5 1.1 %join.1 = bf16[2,2,256]{2,1,0:T(2,128)(2,1)} custom-call(bf16[640,128]{1,0:T(8,128)(2,1)S(1)} %bitcast.9, f32[1,256]{1,0:T(1,128)S(1)} %bitcast.11, bf16[256,256]{1,0:T(8,128)(2,1)S(1)} %copy-done.3), custom_call_target="tpu_custom_call" | custom-call | tf_op jit(solution)/shard_map/join/pallas_call | solution.py:225
  (1 shorter events, 0.0 us)
Async XLA Ops:
  1.4 18.9 %copy-start.6 = (bf16[2,128,256]{2,1,0:T(8,128)(2,1)S(1)}, bf16[2,128,256]{2,1,0:T(8,128)(2,1)}, u32[]{:S(2)}) copy-start(bf16[2,128,256]{2,1,0:T(8,128)(2,1)} %param.9) | copy-start | bytes 393220
  1.4 38.9 %all-to-all-start = ((bf16[64,8,128]{2,1,0:T(8,128)(2,1)}), bf16[64,8,128]{2,1,0:T(8,128)(2,1)S(1)}, u32[]{:S(2)}, u32[]{:S(2)}) async-start(bf16[64,8,128]{2,1,0:T(8,128)(2,1)} %broadcast_in_dim.8), calls=%async_computation | async-start | bytes 262144 | tf_op jit(solution)/shard_map/all_to_all | solution.py:188
  33.6 4.5 %copy-start = (bf16[256,256]{1,0:T(8,128)(2,1)S(1)}, bf16[256,256]{1,0:T(8,128)(2,1)}, u32[]{:S(2)}) copy-start(bf16[256,256]{1,0:T(8,128)(2,1)} %refs_2_.3) | copy-start | bytes 393220
  33.6 4.5 %copy-start.1 = (bf16[256,256]{1,0:T(8,128)(2,1)S(1)}, bf16[256,256]{1,0:T(8,128)(2,1)}, u32[]{:S(2)}) copy-start(bf16[256,256]{1,0:T(8,128)(2,1)} %refs_3_.1) | copy-start | bytes 393220
  33.7 5.5 %collective-permute-start = (bf16[2,2,128,256]{3,2,1,0:T(8,128)(2,1)S(1)}, bf16[2,2,128,256]{3,2,1,0:T(8,128)(2,1)S(1)}, u32[]{:S(2)}, u32[]{:S(2)}) collective-permute-start(bf16[2,2,128,256]{3,2,1,0:T(8,128)(2,1)S(1)} %bitcast.13), channel_id=1, source_target_pairs={{0,1},{1,0},{2,3},{3,2},{4,5},{5,4},{6,7},{7,6},{8,9},{9,8},{10,11... | collective-permute-start | bytes 786440 | tf_op jit(solution)/shard_map/ppermute | solution.py:192
  35.7 2.4 %copy-start.4 = (s32[2]{0:T(128)S(1)}, s32[2]{0:T(128)}, u32[]{:S(2)}) copy-start(s32[2]{0:T(128)} %length_ref.3) | copy-start | bytes 28
  35.8 3.6 %collective-permute-start.1 = (bf16[2,2,128,256]{3,2,1,0:T(8,128)(2,1)S(1)}, bf16[2,2,128,256]{3,2,1,0:T(8,128)(2,1)S(1)}, u32[]{:S(2)}, u32[]{:S(2)}) collective-permute-start(bf16[2,2,128,256]{3,2,1,0:T(8,128)(2,1)S(1)} %bitcast.12), channel_id=1, source_target_pairs={{0,1},{1,0},{2,3},{3,2},{4,5},{5,4},{6,7},{7,6},{8,9},{9,8},{10,11... | collective-permute-start | bytes 786440 | tf_op jit(solution)/shard_map/ppermute | solution.py:192
  39.2 1.1 %copy-start.2 = (bf16[256,256]{1,0:T(8,128)(2,1)S(1)}, bf16[256,256]{1,0:T(8,128)(2,1)}, u32[]{:S(2)}) copy-start(bf16[256,256]{1,0:T(8,128)(2,1)} %wq_ref.1) | copy-start | bytes 393220
  45.3 32.5 %copy-start.3 = (bf16[256,256]{1,0:T(8,128)(2,1)S(1)}, bf16[256,256]{1,0:T(8,128)(2,1)}, u32[]{:S(2)}) copy-start(bf16[256,256]{1,0:T(8,128)(2,1)} %wout_ref.1) | copy-start | bytes 393220
  77.8 0.7 copy-start.5

commit v3 on v2

--- a/solution.py
+++ b/solution.py
@@ -11,6 +11,8 @@
 HEAD_DIM = 32
 LANES = 128
 SLOT = 10
+DEPTH = 16
+FIRSTS = ((1, 12), (1, 4))
 STATS = 64
 EXPONENT = math.log2(math.e) / math.sqrt(HEAD_DIM)
 NT = (((1,), (1,)), ((), ()))
@@ -27,7 +29,8 @@
 
 
 def project_kernel(side, length_ref, *refs):
-    history_refs, (wk_ref, wv_ref, keys_ref, values_ref) = refs[:-4], refs[-4:]
+    history_refs, (wk_ref, wv_ref, gain_ref, keys_ref, values_ref, gain_out) = refs[:-6], refs[-6:]
+    gain_out[...] = gain_ref[...]
     chips, users, block, width = history_refs[0].shape
     rows = len(history_refs) * chips * block
     first_row = lax.axis_index("seq") * 2 * rows
@@ -53,7 +56,7 @@
         values_ref[user] = jnp.where(lane_index < valid, values, 0.0).astype(jnp.bfloat16)
 
 
-def attend_kernel(cand_ref, keys0, values0, keys1, values1, wq_ref, out_ref, cand_wide, out_wide):
+def attend_kernel(runs, cand_ref, keys0, values0, keys1, values1, wq_ref, out_ref, cand_wide, out_wide):
     users, _, width = keys0.shape
     devices = cand_ref.shape[0] // 8
     own = 2
@@ -71,7 +74,13 @@
         candidates = [
             jnp.concatenate(
                 [
-                    cand_wide[pl.ds((user * own + i) * 2 + half, devices, stride=8), :]
+                    jnp.concatenate(
+                        [
+                            cand_wide[pl.ds(8 * start + (user * own + i) * 2 + half, size, stride=8)]
+                            for start, size in runs
+                        ],
+                        axis=0,
+                    )
                     for half in range(2)
                 ],
                 axis=1,
@@ -180,12 +189,36 @@
         out_ref[user] = result[user * own : (user + 1) * own].astype(jnp.bfloat16)
 
 
+def seq_order(count, first):
+    depth = math.gcd(count, DEPTH)
+    breadth = count // depth
+    return [
+        [
+            (y + first[0]) % breadth * depth + (z + first[1]) % depth
+            for y in range(breadth)
+            for z in range(depth)
+        ]
+    ]
+
+
+def runs_of(given, wanted):
+    runs = []
+    for device in wanted:
+        index = given.index(device)
+        if runs and sum(runs[-1]) == index:
+            runs[-1] = (runs[-1][0], runs[-1][1] + 1)
+        else:
+            runs.append((index, 1))
+    return tuple(runs)
+
+
 def shards(seq_count, candidates, history, lengths, w_query, w_key, w_value, norm_gain, w_out):
     users, own, width = candidates.shape
+    there, back = (seq_order(seq_count, first) for first in FIRSTS)
     vmem = pl.BlockSpec(memory_space=pltpu.VMEM)
     smem = pl.BlockSpec(memory_space=pltpu.SMEM)
     copies = jnp.broadcast_to(candidates.reshape(1, 8, LANES), (seq_count, 8, LANES))
-    gathered = lax.all_to_all(copies, "seq", 0, 0, tiled=True).reshape(seq_count * 8, LANES)
+    gathered = lax.all_to_all(copies, "seq", 0, 0, axis_index_groups=there, tiled=True).reshape(seq_count * 8, LANES)
     mine = lax.all_gather(history, "x", axis=0)
     half = mine.shape[0] // 2
     theirs = [
@@ -193,23 +226,24 @@
     ]
     rows = mine.shape[0] * mine.shape[2]
 
-    def project(side, *history):
+    def project(side, gain, *history):
         return pl.pallas_call(
             functools.partial(project_kernel, side),
             out_shape=(
                 jax.ShapeDtypeStruct((users, rows, width), jnp.bfloat16),
                 jax.ShapeDtypeStruct((users, width + ONES, rows), jnp.bfloat16),
+                jax.ShapeDtypeStruct((1, width), jnp.float32),
             ),
-            in_specs=[smem] + [vmem] * (len(history) + 2),
-            out_specs=(vmem, vmem),
+            in_specs=[smem] + [vmem] * (len(history) + 3),
+            out_specs=(vmem, vmem, vmem),
             compiler_params=pltpu.CompilerParams(vmem_limit_bytes=24 * 1024 * 1024),
             name="project",
-        )(lengths, *history, w_key, w_value)
-
-    keys0, values0 = project(0, mine)
-    keys1, values1 = project(1, *theirs)
+        )(lengths, *history, w_key, w_value, gain)
+
+    keys0, values0, gain = project(0, norm_gain.reshape(1, width), mine)
+    keys1, values1, gain = project(1, gain, *theirs)
     partial = pl.pallas_call(
-        attend_kernel,
+        functools.partial(attend_kernel, runs_of(there[0], back[0])),
         out_shape=jax.ShapeDtypeStruct((seq_count * SLOT, LANES), jnp.bfloat16),
         in_specs=[vmem] * 6,
         out_specs=vmem,
@@ -221,7 +255,7 @@
         name="attend",
     )(gathered, keys0, values0, keys1, values1, w_query)
     partial = partial.reshape(seq_count, SLOT // 2, 2, LANES)
-    partial = lax.all_to_all(partial, "seq", 0, 0, tiled=True)
+    partial = lax.all_to_all(partial, "seq", 0, 0, axis_index_groups=back, tiled=True)
     return pl.pallas_call(
         join_kernel,
         out_shape=jax.ShapeDtypeStruct((users, own, width), jnp.bfloat16),
@@ -230,7 +264,7 @@
         scratch_shapes=[pltpu.VMEM((seq_count * SLOT, LANES), jnp.float32)],
         compiler_params=pltpu.CompilerParams(vmem_limit_bytes=16 * 1024 * 1024),
         name="join",
-    )(partial.reshape(seq_count * SLOT, LANES), norm_gain.reshape(1, width), w_out)
+    )(partial.reshape(seq_count * SLOT, LANES), gain, w_out)
 
 
 def solution(mesh):

time: 79.9 us -> 70.7 us (0.88)
  blocking collectives: 45.9 us -> 36.2 us
    all_to_all x1, blocking collectives: 32.5 us -> 22.9 us  [shards(): lax.all_to_all(partial, 'seq', 0, 0, axis_index_groups=back, tiled=True)]
  transfers between devices with their start and end apart: 3 -> 3, of which waited for: 1 -> 0; matrix products, arithmetic and copies ran while one was open for 0% -> 0% of each run, Pallas kernels for 2% -> 3%
where the time goes in v3:
time: 70.7 us; the launch traced here: 70.3 us
  blocking collectives  36.2 us (51%)
  starting transfers between devices  23.8 us (34%)
  Pallas kernels  8.09 us (11%)
  local copies, waits for them, and re-layouts  2.08 us (3%)
    all_to_all x1, blocking collectives, shards(): lax.all_to_all(partial, 'seq', 0, 0, axis_index_groups=back, tiled=True)  22.9 us
    all_to_all x1, starting transfers between devices, shards(): lax.all_to_all(copies, 'seq', 0, 0, axis_index_groups=there, tiled=True)  19.3 us
    all_gather x1, blocking collectives, shards(): mine = lax.all_gather(history, 'x', axis=0)  13.3 us
    pallas_call x1, Pallas kernels, shards(): pl.pallas_call(functools.partial(attend_kernel, runs_of(there[0], back[0]...  4.99 us
    ppermute x2, starting transfers between devices, shards(): lax.ppermute(part, 'core', [(0, 1), (1, 0)])  4.46 us
    pallas_call x2, Pallas kernels, project(): pl.pallas_call(functools.partial(project_kernel, side), out_shape=(jax.Sh...  1.99 us
  transfers between devices with their start and end apart: 3, of which 0 were waited for; matrix products, arithmetic and copies ran while one was open for 0% of the time, Pallas kernels for 3%

profile of v3, /device:TPU:6, one launch (start us, length us, event | category | flops | bytes accessed | tf_op | source)
XLA Modules:
  0.0 70.3 jit_solution(10758037508084219356)
XLA Ops:
  0.0 0.7 broadcast_in_dim.7
  0.7 0.7 broadcast_in_dim.8
  1.4 0.0 copy-start.6
  1.4 19.3 %all-to-all-start = ((bf16[64,8,128]{2,1,0:T(8,128)(2,1)}), bf16[64,8,128]{2,1,0:T(8,128)(2,1)S(1)}, u32[]{:S(2)}, u32[]{:S(2)}) async-start(bf16[64,8,128]{2,1,0:T(8,128)(2,1)} %broadcast_in_dim.8), calls=%async_computation | async-start | bytes 262144 | tf_op jit(solution)/shard_map/all_to_all | solution.py:221
  20.7 0.0 copy-done.6
  20.7 13.3 %all-gather = bf16[8,128,256]{2,1,0:T(8,128)(2,1)S(1)} all-gather(bf16[2,128,256]{2,1,0:T(8,128)(2,1)S(1)} %copy-done.6), channel_id=2, replica_groups=mesh['seq'=64,'x'=4,'core'=2] {'x'}, dimensions={0}, use_global_device_ids=true | all-gather | bytes 655360 | tf_op jit(solution)/shard_map/all_gather | solution.py:222
  34.0 0.0 copy-start
  34.0 0.0 copy-start.1
  34.1 2.1 %collective-permute-start = (bf16[2,2,128,256]{3,2,1,0:T(8,128)(2,1)S(1)}, bf16[2,2,128,256]{3,2,1,0:T(8,128)(2,1)S(1)}, u32[]{:S(2)}, u32[]{:S(2)}) collective-permute-start(bf16[2,2,128,256]{3,2,1,0:T(8,128)(2,1)S(1)} %bitcast.13), channel_id=1, source_target_pairs={{0,1},{1,0},{2,3},{3,2},{4,5},{5,4},{6,7},{7,6},{8,9},{9,8},{10,11... | collective-permute-start | bytes 786440 | tf_op jit(solution)/shard_map/ppermute | solution.py:225
  36.1 2.4 %collective-permute-start.1 = (bf16[2,2,128,256]{3,2,1,0:T(8,128)(2,1)S(1)}, bf16[2,2,128,256]{3,2,1,0:T(8,128)(2,1)S(1)}, u32[]{:S(2)}, u32[]{:S(2)}) collective-permute-start(bf16[2,2,128,256]{3,2,1,0:T(8,128)(2,1)S(1)} %bitcast.12), channel_id=1, source_target_pairs={{0,1},{1,0},{2,3},{3,2},{4,5},{5,4},{6,7},{7,6},{8,9},{9,8},{10,11... | collective-permute-start | bytes 786440 | tf_op jit(solution)/shard_map/ppermute | solution.py:225
  38.6 0.0 copy-start.4
  38.6 0.0 copy-start.5
  38.6 0.0 copy-done
  38.6 0.0 copy-done.1
  38.6 0.6 copy-done.4
  39.2 0.0 copy-done.5
  39.3 1.0 %project.2 = (bf16[2,512,256]{2,1,0:T(8,128)(2,1)S(1)}, bf16[2,272,512]{2,1,0:T(8,128)(2,1)S(1)}, f32[1,256]{1,0:T(1,128)S(1)}) custom-call(s32[2]{0:T(128)S(1)} %copy-done.4, bf16[4,2,128,256]{3,2,1,0:T(8,128)(2,1)S(1)} %bitcast.7, bf16[256,256]{1,0:T(8,128)(2,1)S(1)} %copy-done, bf16[256,256]{1,0:T(8,128)(2,1)S(1)} %copy-done.1, f32[1,256]{1,0:T(1,128)S(1)} %bitcast.11), custom_call_target="tpu_custom_call" | custom-call | tf_op jit(solution)/shard_map/project/pallas_call | solution.py:230
  40.3 0.0 collective-permute-done.refs_0_
  40.3 0.0 collective-permute-done.1.refs_1_
  40.3 0.0 copy-start.2
  40.3 1.0 %project.3 = (bf16[2,512,256]{2,1,0:T(8,128)(2,1)S(1)}, bf16[2,272,512]{2,1,0:T(8,128)(2,1)S(1)}, f32[1,256]{1,0:T(1,128)S(1)}) custom-call(s32[2]{0:T(128)S(1)} %copy-done.4, bf16[2,2,128,256]{3,2,1,0:T(8,128)(2,1)S(1)} %collective-permute-done.refs_0_, bf16[2,2,128,256]{3,2,1,0:T(8,128)(2,1)S(1)} %collective-permute-done.1.refs_1_, ...), custom_call_target="tpu_custom_call" | custom-call | tf_op jit(solution)/shard_map/project/pallas_call | solution.py:230
  41.3 0.0 all-to-all-done
  41.3 0.0 copy-done.2
  41.3 5.0 %attend.1 = bf16[640,128]{1,0:T(8,128)(2,1)S(1)} custom-call(bf16[512,128]{1,0:T(8,128)(2,1)S(1)} %bitcast.10, bf16[2,512,256]{2,1,0:T(8,128)(2,1)S(1)} %get-tuple-element.11.keys0, bf16[2,272,512]{2,1,0:T(8,128)(2,1)S(1)} %get-tuple-element.12.values0, bf16[2,512,256]{2,1,0:T(8,128)(2,1)S(1)} %get-tuple-element.14.keys1, ...), custom_call_target="tpu_custom_call" | custom-call | tf_op jit(solution)/shard_map/attend/pallas_call | solution.py:245
  46.3 0.0 copy-start.3
  46.3 22.9 %all_to_all.10 = bf16[64,5,2,128]{3,2,1,0:T(2,128)(2,1)S(1)} all-to-all(bf16[64,5,2,128]{3,2,1,0:T(2,128)(2,1)S(1)} %bitcast.8), channel_id=1, replica_groups={{160,168,176,184,192,200,208,216,224,232,240,248,128,136,144,152,288,29..., dimensions={0} | all-to-all | bytes 327680 | tf_op jit(solution)/shard_map/all_to_all | solution.py:258
  69.2 0.0 copy-done.3
  69.2 1.1 %join.1 = bf16[2,2,256]{2,1,0:T(2,128)(2,1)} custom-call(bf16[640,128]{1,0:T(8,128)(2,1)S(1)} %bitcast.9, f32[1,256]{1,0:T(1,128)S(1)} %get-tuple-element.16.gain_ref, bf16[256,256]{1,0:T(8,128)(2,1)S(1)} %copy-done.3), custom_call_target="tpu_custom_call" | custom-call | tf_op jit(solution)/shard_map/join/pallas_call | solution.py:259
  (1 shorter events, 0.0 us)
Async XLA Ops:
  1.4 19.3 %copy-start.6 = (bf16[2,128,256]{2,1,0:T(8,128)(2,1)S(1)}, bf16[2,128,256]{2,1,0:T(8,128)(2,1)}, u32[]{:S(2)}) copy-start(bf16[2,128,256]{2,1,0:T(8,128)(2,1)} %param.9) | copy-start | bytes 393220
  1.4 39.9 %all-to-all-start = ((bf16[64,8,128]{2,1,0:T(8,128)(2,1)}), bf16[64,8,128]{2,1,0:T(8,128)(2,1)S(1)}, u32[]{:S(2)}, u32[]{:S(2)}) async-start(bf16[64,8,128]{2,1,0:T(8,128)(2,1)} %broadcast_in_dim.8), calls=%async_computation | async-start | bytes 262144 | tf_op jit(solution)/shard_map/all_to_all | solution.py:221
  34.0 4.5 %copy-start = (bf16[256,256]{1,0:T(8,128)(2,1)S(1)}, bf16[256,256]{1,0:T(8,128)(2,1)}, u32[]{:S(2)}) copy-start(bf16[256,256]{1,0:T(8,128)(2,1)} %refs_2_.3) | copy-start | bytes 393220
  34.0 4.6 %copy-start.1 = (bf16[256,256]{1,0:T(8,128)(2,1)S(1)}, bf16[256,256]{1,0:T(8,128)(2,1)}, u32[]{:S(2)}) copy-start(bf16[256,256]{1,0:T(8,128)(2,1)} %refs_3_.1) | copy-start | bytes 393220
  34.1 6.2 %collective-permute-start = (bf16[2,2,128,256]{3,2,1,0:T(8,128)(2,1)S(1)}, bf16[2,2,128,256]{3,2,1,0:T(8,128)(2,1)S(1)}, u32[]{:S(2)}, u32[]{:S(2)}) collective-permute-start(bf16[2,2,128,256]{3,2,1,0:T(8,128)(2,1)S(1)} %bitcast.13), channel_id=1, source_target_pairs={{0,1},{1,0},{2,3},{3,2},{4,5},{5,4},{6,7},{7,6},{8,9},{9,8},{10,11... | collective-permute-start | bytes 786440 | tf_op jit(solution)/shard_map/ppermute | solution.py:225
  36.1 4.1 %collective-permute-start.1 = (bf16[2,2,128,256]{3,2,1,0:T(8,128)(2,1)S(1)}, bf16[2,2,128,256]{3,2,1,0:T(8,128)(2,1)S(1)}, u32[]{:S(2)}, u32[]{:S(2)}) collective-permute-start(bf16[2,2,128,256]{3,2,1,0:T(8,128)(2,1)S(1)} %bitcast.12), channel_id=1, source_target_pairs={{0,1},{1,0},{2,3},{3,2},{4,5},{5,4},{6,7},{7,6},{8,9},{9,8},{10,11... | collective-permute-start | bytes 786440 | tf_op jit(solution)/shard_map/ppermute | solution.py:225
  38.6 0.7 copy-start.4
  38.6 0.7 copy-start.5
  40.3 1.0 %copy-start.2 = (bf16[256,256]{1,0:T(8,128)(2,1)S(1)}, bf16[256,256]{1,0:T(8,128)(2,1)}, u32[]{:S(2)}) copy-start(bf16[256,256]{1,0:T(8,128)(2,1)} %wq_ref.1) | copy-start | bytes 393220
  46.3 22.9 %copy-start.3 = (bf16[256,256]{1,0:T(8,128)(2,1)S(1)}, bf16[256,256]{1,0:T(8,128)(2,1)}, u32[]{:S(2)}) copy-start(bf16[256,256]{1,0:T(8,128)(2,1)} %wout_ref.1) | copy-start | bytes 393220

commit v4 on v3

--- a/solution.py
+++ b/solution.py
@@ -12,7 +12,7 @@
 LANES = 128
 SLOT = 10
 DEPTH = 16
-FIRSTS = ((1, 12), (1, 4))
+FIRSTS = ((2, 12), (1, 4))
 STATS = 64
 EXPONENT = math.log2(math.e) / math.sqrt(HEAD_DIM)
 NT = (((1,), (1,)), ((), ()))
@@ -29,8 +29,12 @@
 
 
 def project_kernel(side, length_ref, *refs):
-    history_refs, (wk_ref, wv_ref, gain_ref, keys_ref, values_ref, gain_out) = refs[:-6], refs[-6:]
-    gain_out[...] = gain_ref[...]
+    if side:
+        *refs, gain_ref, keys_ref, values_ref, gain_out = refs
+        gain_out[...] = gain_ref[...]
+    else:
+        *refs, keys_ref, values_ref = refs
+    *history_refs, wk_ref, wv_ref = refs
     chips, users, block, width = history_refs[0].shape
     rows = len(history_refs) * chips * block
     first_row = lax.axis_index("seq") * 2 * rows
@@ -64,6 +68,7 @@
     cands = devices * own
     cand_wide[...] = cand_ref[...].astype(jnp.float32)
     head_of_lane = lax.broadcasted_iota(jnp.int32, (cands, width), 1) // HEAD_DIM
+    all_keys, all_queries = [], []
     for user in range(users):
         halves = [(keys0, values0), (keys1, values1)]
         any_valid = [values[user, width : width + 1, 0:1] > 0.0 for _, values in halves]
@@ -90,36 +95,50 @@
         candidates = jnp.concatenate(candidates, axis=0).astype(jnp.bfloat16)
         queries = jnp.dot(candidates, wq_ref[...], preferred_element_type=jnp.float32)
         queries = queries.astype(jnp.bfloat16).astype(jnp.float32)
-        numerators, peaks, totals = [], [], []
-        for pair in range(heads // 2):
-            both = jnp.concatenate(
+        all_keys.append(keys)
+        all_queries.append(queries)
+
+    def scores_of(user, pair):
+        both = jnp.concatenate(
+            [
+                jnp.where(head_of_lane == 2 * pair + k, all_queries[user], 0.0).astype(jnp.bfloat16)
+                for k in range(2)
+            ],
+            axis=0,
+        )
+        return [
+            lax.dot_general(part, both, NT, preferred_element_type=jnp.float32)
+            for part in all_keys[user]
+        ]
+
+    steps = [(user, pair) for user in range(users) for pair in range(heads // 2)]
+    ahead = [scores_of(*step) for step in steps[:2]]
+    for step, (user, pair) in enumerate(steps):
+        if step + 2 < len(steps):
+            ahead.append(scores_of(*steps[step + 2]))
+        scores = ahead.pop(0)
+        halves = [(keys0, values0), (keys1, values1)]
+        if pair == 0:
+            numerators, peaks, totals = [], [], []
+        peak = jnp.max(jnp.maximum(scores[0], scores[1]), axis=0, keepdims=True)
+        sums = 0.0
+        for part, (_, values) in zip(scores, halves):
+            exps = jnp.exp2((part - peak) * EXPONENT).astype(jnp.bfloat16)
+            pair_values = jnp.concatenate(
                 [
-                    jnp.where(head_of_lane == 2 * pair + k, queries, 0.0).astype(jnp.bfloat16)
-                    for k in range(2)
+                    values[user, 2 * pair * HEAD_DIM : 2 * (pair + 1) * HEAD_DIM],
+                    values[user, width:],
                 ],
                 axis=0,
             )
-            scores = [
-                lax.dot_general(part, both, NT, preferred_element_type=jnp.float32)
-                for part in keys
-            ]
-            peak = jnp.max(jnp.maximum(scores[0], scores[1]), axis=0, keepdims=True)
-            sums = 0.0
-            for part, (_, values) in zip(scores, halves):
-                exps = jnp.exp2((part - peak) * EXPONENT).astype(jnp.bfloat16)
-                pair_values = jnp.concatenate(
-                    [
-                        values[user, 2 * pair * HEAD_DIM : 2 * (pair + 1) * HEAD_DIM],
-                        values[user, width:],
-                    ],
-                    axis=0,
-                )
-                sums += jnp.dot(pair_values, exps, preferred_element_type=jnp.float32)
-            for k in range(2):
-                lanes = slice(k * cands, (k + 1) * cands)
-                numerators.append(sums[k * HEAD_DIM : (k + 1) * HEAD_DIM, lanes])
-                peaks.append(peak[:, lanes])
-                totals.append(sums[2 * HEAD_DIM : 2 * HEAD_DIM + 1, lanes])
+            sums += jnp.dot(pair_values, exps, preferred_element_type=jnp.float32)
+        for k in range(2):
+            lanes = slice(k * cands, (k + 1) * cands)
+            numerators.append(sums[k * HEAD_DIM : (k + 1) * HEAD_DIM, lanes])
+            peaks.append(peak[:, lanes])
+            totals.append(sums[2 * HEAD_DIM : 2 * HEAD_DIM + 1, lanes])
+        if pair < heads // 2 - 1:
+            continue
         total = jnp.concatenate(totals, axis=0)
         peak = jnp.where(total > 0.0, jnp.concatenate(peaks, axis=0), -1e30)
         pieces = parts_of(peak, 3) + parts_of(total, 2)
@@ -226,22 +245,24 @@
     ]
     rows = mine.shape[0] * mine.shape[2]
 
-    def project(side, gain, *history):
+    def project(side, *operands):
+        shapes = [
+            jax.ShapeDtypeStruct((users, rows, width), jnp.bfloat16),
+            jax.ShapeDtypeStruct((users, width + ONES, rows), jnp.bfloat16),
+        ]
+        if side:
+            shapes.append(jax.ShapeDtypeStruct((1, width), jnp.float32))
         return pl.pallas_call(
             functools.partial(project_kernel, side),
-            out_shape=(
-                jax.ShapeDtypeStruct((users, rows, width), jnp.bfloat16),
-                jax.ShapeDtypeStruct((users, width + ONES, rows), jnp.bfloat16),
-                jax.ShapeDtypeStruct((1, width), jnp.float32),
-            ),
-            in_specs=[smem] + [vmem] * (len(history) + 3),
-            out_specs=(vmem, vmem, vmem),
+            out_shape=shapes,
+            in_specs=[smem] + [vmem] * len(operands),
+            out_specs=[vmem] * len(shapes),
             compiler_params=pltpu.CompilerParams(vmem_limit_bytes=24 * 1024 * 1024),
             name="project",
-        )(lengths, *history, w_key, w_value, gain)
-
-    keys0, values0, gain = project(0, norm_gain.reshape(1, width), mine)
-    keys1, values1, gain = project(1, gain, *theirs)
+        )(lengths, *operands)
+
+    keys0, values0 = project(0, mine, w_key, w_value)
+    keys1, values1, gain = project(1, *theirs, w_key, w_value, norm_gain.reshape(1, width))
     partial = pl.pallas_call(
         functools.partial(attend_kernel, runs_of(there[0], back[0])),
         out_shape=jax.ShapeDtypeStruct((seq_count * SLOT, LANES), jnp.bfloat16),

time: 70.7 us -> 68 us (0.962)
  Pallas kernels: 8.09 us -> 6.32 us
  blocking collectives: 36.2 us -> 34.8 us
    pallas_call x1, Pallas kernels: 4.99 us -> 3.22 us  [shards(): pl.pallas_call(functools.partial(attend_kernel, runs_of(there[0], back[0]...]
    all_to_all x1, blocking collectives: 22.9 us -> 21.5 us  [shards(): lax.all_to_all(partial, 'seq', 0, 0, axis_index_groups=back, tiled=True)]
  transfers between devices with their start and end apart: 3 -> 3, of which waited for: 0 -> 1; matrix products, arithmetic and copies ran while one was open for 0% -> 0% of each run, Pallas kernels for 3% -> 3%
where the time goes in v4:
time: 68 us; the launch traced here: 67.6 us
  blocking collectives  34.8 us (51%)
  starting transfers between devices  24.3 us (36%)
  Pallas kernels  6.32 us (9%)
  local copies, waits for them, and re-layouts  2 us (3%)
    all_to_all x1, blocking collectives, shards(): lax.all_to_all(partial, 'seq', 0, 0, axis_index_groups=back, tiled=True)  21.5 us
    all_to_all x1, starting transfers between devices, shards(): lax.all_to_all(copies, 'seq', 0, 0, axis_index_groups=there, tiled=True)  19.8 us
    all_gather x1, blocking collectives, shards(): mine = lax.all_gather(history, 'x', axis=0)  13.3 us
    ppermute x2, starting transfers between devices, shards(): lax.ppermute(part, 'core', [(0, 1), (1, 0)])  4.46 us
    pallas_call x1, Pallas kernels, shards(): pl.pallas_call(functools.partial(attend_kernel, runs_of(there[0], back[0]...  3.22 us
    pallas_call x2, Pallas kernels, project(): pl.pallas_call(functools.partial(project_kernel, side), out_shape=shapes,...  1.98 us
    broadcast_in_dim x2, local copies, waits for them, and re-layouts, shards(): jnp.broadcast_to(candidates.reshape(1, 8, LANES), (seq_count, 8, LANES))  1.36 us
  transfers between devices with their start and end apart: 3, of which 1 were waited for; matrix products, arithmetic and copies ran while one was open for 0% of the time, Pallas kernels for 3%

profile of v4, /device:TPU:6, one launch (start us, length us, event | category | flops | bytes accessed | tf_op | source)
XLA Modules:
  0.0 67.6 jit_solution(1510757082427761616)
XLA Ops:
  0.0 0.7 %broadcast_in_dim.7 = bf16[8,128]{1,0:T(8,128)(2,1)S(1)} reshape(bf16[2,2,256]{2,1,0:T(2,128)(2,1)} %param.8) | data formatting | bytes 4096 | tf_op jit(solution)/shard_map/broadcast_in_dim | solution.py:239
  0.7 0.7 broadcast_in_dim.8
  1.4 0.0 copy-start.6
  1.4 19.8 %all-to-all-start = ((bf16[64,8,128]{2,1,0:T(8,128)(2,1)}), bf16[64,8,128]{2,1,0:T(8,128)(2,1)S(1)}, u32[]{:S(2)}, u32[]{:S(2)}) async-start(bf16[64,8,128]{2,1,0:T(8,128)(2,1)} %broadcast_in_dim.8), calls=%async_computation | async-start | bytes 262144 | tf_op jit(solution)/shard_map/all_to_all | solution.py:240
  21.2 0.0 copy-done.6
  21.2 13.3 %all-gather = bf16[8,128,256]{2,1,0:T(8,128)(2,1)S(1)} all-gather(bf16[2,128,256]{2,1,0:T(8,128)(2,1)S(1)} %copy-done.6), channel_id=2, replica_groups=mesh['seq'=64,'x'=4,'core'=2] {'x'}, dimensions={0}, use_global_device_ids=true | all-gather | bytes 655360 | tf_op jit(solution)/shard_map/all_gather | solution.py:241
  34.5 0.0 copy-start
  34.5 0.0 copy-start.1
  34.6 2.1 %collective-permute-start = (bf16[2,2,128,256]{3,2,1,0:T(8,128)(2,1)S(1)}, bf16[2,2,128,256]{3,2,1,0:T(8,128)(2,1)S(1)}, u32[]{:S(2)}, u32[]{:S(2)}) collective-permute-start(bf16[2,2,128,256]{3,2,1,0:T(8,128)(2,1)S(1)} %bitcast.13), channel_id=1, source_target_pairs={{0,1},{1,0},{2,3},{3,2},{4,5},{5,4},{6,7},{7,6},{8,9},{9,8},{10,11... | collective-permute-start | bytes 786440 | tf_op jit(solution)/shard_map/ppermute | solution.py:244
  36.6 0.0 copy-start.4
  36.7 2.4 %collective-permute-start.1 = (bf16[2,2,128,256]{3,2,1,0:T(8,128)(2,1)S(1)}, bf16[2,2,128,256]{3,2,1,0:T(8,128)(2,1)S(1)}, u32[]{:S(2)}, u32[]{:S(2)}) collective-permute-start(bf16[2,2,128,256]{3,2,1,0:T(8,128)(2,1)S(1)} %bitcast.12), channel_id=1, source_target_pairs={{0,1},{1,0},{2,3},{3,2},{4,5},{5,4},{6,7},{7,6},{8,9},{9,8},{10,11... | collective-permute-start | bytes 786440 | tf_op jit(solution)/shard_map/ppermute | solution.py:244
  39.1 0.0 copy-done
  39.1 0.0 copy-done.1
  39.1 0.0 copy-done.4
  39.1 1.0 %project.2 = (bf16[2,512,256]{2,1,0:T(8,128)(2,1)S(1)}, bf16[2,272,512]{2,1,0:T(8,128)(2,1)S(1)}) custom-call(s32[2]{0:T(128)S(1)} %copy-done.4, bf16[4,2,128,256]{3,2,1,0:T(8,128)(2,1)S(1)} %bitcast.7, bf16[256,256]{1,0:T(8,128)(2,1)S(1)} %copy-done, bf16[256,256]{1,0:T(8,128)(2,1)S(1)} %copy-done.1), custom_call_target="tpu_custom_call" | custom-call | tf_op jit(solution)/shard_map/project/pallas_call | solution.py:255
  40.1 0.0 copy-start.5
  40.1 0.0 collective-permute-done.refs_0_
  40.1 0.1 collective-permute-done.1.refs_1_
  40.2 0.6 copy-done.5
  40.8 0.0 copy-start.2
  40.8 1.0 %project.3 = (bf16[2,512,256]{2,1,0:T(8,128)(2,1)S(1)}, bf16[2,272,512]{2,1,0:T(8,128)(2,1)S(1)}, f32[1,256]{1,0:T(1,128)S(1)}) custom-call(s32[2]{0:T(128)S(1)} %copy-done.4, bf16[2,2,128,256]{3,2,1,0:T(8,128)(2,1)S(1)} %collective-permute-done.refs_0_, bf16[2,2,128,256]{3,2,1,0:T(8,128)(2,1)S(1)} %collective-permute-done.1.refs_1_, ...), custom_call_target="tpu_custom_call" | custom-call | tf_op jit(solution)/shard_map/project/pallas_call | solution.py:255
  41.8 0.0 all-to-all-done
  41.8 0.0 copy-done.2
  41.8 3.2 %attend.1 = bf16[640,128]{1,0:T(8,128)(2,1)S(1)} custom-call(bf16[512,128]{1,0:T(8,128)(2,1)S(1)} %bitcast.10, bf16[2,512,256]{2,1,0:T(8,128)(2,1)S(1)} %get-tuple-element.10.keys0, bf16[2,272,512]{2,1,0:T(8,128)(2,1)S(1)} %get-tuple-element.11.values0, bf16[2,512,256]{2,1,0:T(8,128)(2,1)S(1)} %get-tuple-element.12.keys1, ...), custom_call_target="tpu_custom_call" | custom-call | tf_op jit(solution)/shard_map/attend/pallas_call | solution.py:266
  45.0 0.0 copy-start.3
  45.0 21.5 %all_to_all.10 = bf16[64,5,2,128]{3,2,1,0:T(2,128)(2,1)S(1)} all-to-all(bf16[64,5,2,128]{3,2,1,0:T(2,128)(2,1)S(1)} %bitcast.8), channel_id=1, replica_groups={{160,168,176,184,192,200,208,216,224,232,240,248,128,136,144,152,288,29..., dimensions={0} | all-to-all | bytes 327680 | tf_op jit(solution)/shard_map/all_to_all | solution.py:279
  66.5 0.0 copy-done.3
  66.5 1.1 %join.1 = bf16[2,2,256]{2,1,0:T(2,128)(2,1)} custom-call(bf16[640,128]{1,0:T(8,128)(2,1)S(1)} %bitcast.9, f32[1,256]{1,0:T(1,128)S(1)} %get-tuple-element.14.gain_ref, bf16[256,256]{1,0:T(8,128)(2,1)S(1)} %copy-done.3), custom_call_target="tpu_custom_call" | custom-call | tf_op jit(solution)/shard_map/join/pallas_call | solution.py:280
  (1 shorter events, 0.0 us)
Async XLA Ops:
  1.4 19.8 %copy-start.6 = (bf16[2,128,256]{2,1,0:T(8,128)(2,1)S(1)}, bf16[2,128,256]{2,1,0:T(8,128)(2,1)}, u32[]{:S(2)}) copy-start(bf16[2,128,256]{2,1,0:T(8,128)(2,1)} %param.9) | copy-start | bytes 393220
  1.4 40.4 %all-to-all-start = ((bf16[64,8,128]{2,1,0:T(8,128)(2,1)}), bf16[64,8,128]{2,1,0:T(8,128)(2,1)S(1)}, u32[]{:S(2)}, u32[]{:S(2)}) async-start(bf16[64,8,128]{2,1,0:T(8,128)(2,1)} %broadcast_in_dim.8), calls=%async_computation | async-start | bytes 262144 | tf_op jit(solution)/shard_map/all_to_all | solution.py:240
  34.5 4.5 %copy-start = (bf16[256,256]{1,0:T(8,128)(2,1)S(1)}, bf16[256,256]{1,0:T(8,128)(2,1)}, u32[]{:S(2)}) copy-start(bf16[256,256]{1,0:T(8,128)(2,1)} %refs_2_.3) | copy-start | bytes 393220
  34.5 4.5 %copy-start.1 = (bf16[256,256]{1,0:T(8,128)(2,1)S(1)}, bf16[256,256]{1,0:T(8,128)(2,1)}, u32[]{:S(2)}) copy-start(bf16[256,256]{1,0:T(8,128)(2,1)} %refs_3_.1) | copy-start | bytes 393220
  34.6 5.5 %collective-permute-start = (bf16[2,2,128,256]{3,2,1,0:T(8,128)(2,1)S(1)}, bf16[2,2,128,256]{3,2,1,0:T(8,128)(2,1)S(1)}, u32[]{:S(2)}, u32[]{:S(2)}) collective-permute-start(bf16[2,2,128,256]{3,2,1,0:T(8,128)(2,1)S(1)} %bitcast.13), channel_id=1, source_target_pairs={{0,1},{1,0},{2,3},{3,2},{4,5},{5,4},{6,7},{7,6},{8,9},{9,8},{10,11... | collective-permute-start | bytes 786440 | tf_op jit(solution)/shard_map/ppermute | solution.py:244
  36.6 2.4 %copy-start.4 = (s32[2]{0:T(128)S(1)}, s32[2]{0:T(128)}, u32[]{:S(2)}) copy-start(s32[2]{0:T(128)} %length_ref.3) | copy-start | bytes 28
  36.7 3.6 %collective-permute-start.1 = (bf16[2,2,128,256]{3,2,1,0:T(8,128)(2,1)S(1)}, bf16[2,2,128,256]{3,2,1,0:T(8,128)(2,1)S(1)}, u32[]{:S(2)}, u32[]{:S(2)}) collective-permute-start(bf16[2,2,128,256]{3,2,1,0:T(8,128)(2,1)S(1)} %bitcast.12), channel_id=1, source_target_pairs={{0,1},{1,0},{2,3},{3,2},{4,5},{5,4},{6,7},{7,6},{8,9},{9,8},{10,11... | collective-permute-start | bytes 786440 | tf_op jit(solution)/shard_map/ppermute | solution.py:244
  40.1 0.7 %copy-start.5 = (f32[256]{0:T(256)S(1)}, f32[256]{0:T(256)}, u32[]{:S(2)}) copy-start(f32[256]{0:T(256)} %param.14) | copy-start | bytes 3076
  40.8 1.0 %copy-start.2 = (bf16[256,256]{1,0:T(8,128)(2,1)S(1)}, bf16[256,256]{1,0:T(8,128)(2,1)}, u32[]{:S(2)}) copy-start(bf16[256,256]{1,0:T(8,128)(2,1)} %wq_ref.1) | copy-start | bytes 393220
  45.0 21.5 %copy-start.3 = (bf16[256,256]{1,0:T(8,128)(2,1)S(1)}, bf16[256,256]{1,0:T(8,128)(2,1)}, u32[]{:S(2)}) copy-start(bf16[256,256]{1,0:T(8,128)(2,1)} %wout_ref.1) | copy-start | bytes 393220
